TPU v7x, 512 devices: a whole 4x4x16 slice. The times are simulated.
512 devices in a mesh: tower: 2 (over core), blk: 128 (over x, y_hi, z), mdl: 2 (over y_lo).
Axes of the slice: x: 4, y: 4 (y_hi: 2, y_lo: 2; y = y_hi * 2 + y_lo), z: 16, core: 2. Of those that a mesh axis runs over, the one named last changes fastest.
Arguments:
- embeddings: bfloat16 [2, 1024, 4096], P('tower', 'blk', 'mdl'), may hold values from -120 to 120
- pos_index: int32 [1024, 4], P('blk'), may hold values from 0 to 1023
- pos_count: int32 [1024], P('blk'), may hold values from 1 to 4
- hidden_in: bfloat16 [2, 1024, 4096], P('tower', 'blk', 'mdl'), may hold values from -6 to 6
- w_gate: bfloat16 [2, 14336, 4096], P('tower', 'blk', 'mdl'), may hold values from -0.09375 to 0.09375
- w_up: bfloat16 [2, 14336, 4096], P('tower', 'blk', 'mdl'), may hold values from -0.09375 to 0.09375
- w_down: bfloat16 [2, 14336, 4096], P('tower', 'blk', 'mdl'), may hold values from -0.046875 to 0.046875
Outputs:
- emb_grad: float32 [2, 1024, 4096], P('tower', 'blk', 'mdl')
- grad_gate: bfloat16 [2, 14336, 4096], P('tower', 'blk', 'mdl')
- grad_up: bfloat16 [2, 14336, 4096], P('tower', 'blk', 'mdl')
- grad_down: bfloat16 [2, 14336, 4096], P('tower', 'blk', 'mdl')
Inputs may be any that keep to these rules, and one draw needn't show every extreme that they name: `pos_index`: only the first pos_count slots of a goal's list are used; a list may name a premise more than once.
All inputs are finite; a program needn't handle non-finite values.
Results may differ from a plain program's by a relative error of at most 0.011.
Values may be sent and summed in bfloat16 or wider, within the bound.
A program may use at most 64 MiB of HBM per device.

v0:
```python
import jax
import jax.numpy as jnp
from jax import lax
from jax.sharding import PartitionSpec as P

D = 4096
SEQ = 128
KPOS = 4


LOSS_SCALE = 256.0


def swapped(block, axis, stride):
    count = lax.axis_size(axis)
    route = []
    for low in range(count):
        high = low | 1 << stride
        if high != low and high < count:
            route += [(low, high), (high, low)]
    return lax.ppermute(block, axis, route)


def from_behind(block, axis, distance):
    devices = range(lax.axis_size(axis))
    route = [(i - distance, i) for i in devices if i - distance in devices]
    return lax.ppermute(block, axis, route)


def broadcast(block, axis, holder):
    block = jnp.where(lax.axis_index(axis) == holder, block, jnp.zeros_like(block))
    return lax.psum(block, axis)


def positive_table(index_rows, count_rows, column_ids):
    slot_ids = jnp.arange(KPOS, dtype=jnp.int32)
    live_slots = slot_ids[None, :, None] < count_rows[:, None, None]
    matched = (index_rows[:, :, None] == column_ids[None, None, :]) & live_slots
    hits = jnp.sum(jnp.where(matched, jnp.float32(1.0), jnp.float32(0.0)), axis=1)
    return hits / count_rows[:, None].astype(jnp.float32)


def on_device(embeddings, pos_index, pos_count, hidden_in, w_gate, w_up, w_down):
    contract = (((1,), (1,)), ((), ()))
    own_rows = embeddings[0]
    row_count = own_rows.shape[0]
    total_rows = row_count * lax.axis_size("blk")
    is_goal = lax.axis_index("tower") == 0
    first_row = lax.axis_index("blk") * row_count
    score_scale = D ** (-0.5)
    grad_scale = LOSS_SCALE * score_scale
    partner = swapped(own_rows, "tower", 0)
    others = lax.all_gather(partner, "blk", axis=0, tiled=True)
    partial_scores = lax.dot_general(own_rows, others, contract, preferred_element_type=jnp.float32)
    scores = lax.psum(partial_scores, "mdl") * score_scale
    row_top = jnp.max(scores, axis=1, keepdims=True)
    row_lse = row_top[:, 0] + jnp.log(jnp.sum(jnp.exp(scores - row_top), axis=1))
    lse_blocks = lax.all_gather(row_lse, "blk", axis=0, tiled=True)
    column_lse = from_behind(lse_blocks, "tower", 1)
    all_lists, all_counts = (
        lax.all_gather(pos_index, "blk", axis=0, tiled=True),
        lax.all_gather(pos_count, "blk", axis=0, tiled=True),
    )
    column_ids = jnp.arange(total_rows, dtype=jnp.int32)
    my_rows = first_row + jnp.arange(row_count, dtype=jnp.int32)
    row_weights = positive_table(pos_index, pos_count, column_ids)
    column_weights = positive_table(all_lists, all_counts, my_rows)
    positive = jnp.where(is_goal, row_weights, column_weights.T)
    lse_shift = jnp.where(is_goal, row_lse[:, None], column_lse[None, :])
    coefficient = (jnp.exp(scores - lse_shift) - positive).astype(jnp.bfloat16)
    emb_half = grad_scale * jnp.dot(coefficient, others, preferred_element_type=jnp.float32)
    out_rows = (emb_half / SEQ).astype(jnp.bfloat16)
    micro_batch = broadcast(out_rows, "blk", 0)
    tokens_all = lax.all_gather(hidden_in[0], "blk", axis=0, tiled=True)
    gate_weight = w_gate[0]
    up_weight = w_up[0]
    down_weight = w_down[0]
    gate_part = lax.dot_general(
        gate_weight, tokens_all, contract, preferred_element_type=jnp.float32
    )
    up_part = lax.dot_general(up_weight, tokens_all, contract, preferred_element_type=jnp.float32)
    gate_value, up_value = lax.psum((gate_part, up_part), "mdl")
    back_part = lax.dot_general(
        down_weight, micro_batch, contract, preferred_element_type=jnp.float32
    )
    back_rows = lax.psum(back_part, "mdl")
    unit_count = gate_value.shape[0]
    sigmoid_gate = jax.nn.sigmoid(gate_value)
    activated = gate_value * sigmoid_gate
    hidden = (activated * up_value).astype(jnp.bfloat16)
    back_tokens = jnp.broadcast_to(back_rows[:, :, None], (unit_count, row_count, SEQ)).reshape(
        unit_count, row_count * SEQ
    )
    slope = sigmoid_gate * (1.0 + gate_value * (1.0 - sigmoid_gate))
    gate_back = (back_tokens * up_value * slope).astype(jnp.bfloat16)
    up_back = (back_tokens * activated).astype(jnp.bfloat16)
    grad_gate = jnp.dot(gate_back, tokens_all, preferred_element_type=jnp.float32).astype(
        jnp.bfloat16
    )
    grad_up = jnp.dot(up_back, tokens_all, preferred_element_type=jnp.float32).astype(jnp.bfloat16)
    pooled = jnp.sum(hidden.astype(jnp.float32).reshape(unit_count, row_count, SEQ), axis=2)
    grad_down = jnp.dot(
        pooled, micro_batch.astype(jnp.float32), precision=lax.Precision.HIGHEST
    ).astype(jnp.bfloat16)
    return (emb_half[None], grad_gate[None], grad_up[None], grad_down[None])


def solution(mesh):
    in_specs = (
        P("tower", "blk", "mdl"),
        P("blk", None),
        P("blk"),
        P("tower", "blk", "mdl"),
        P("tower", "blk", "mdl"),
        P("tower", "blk", "mdl"),
        P("tower", "blk", "mdl"),
    )
    out_specs = (
        P("tower", "blk", "mdl"),
        P("tower", "blk", "mdl"),
        P("tower", "blk", "mdl"),
        P("tower", "blk", "mdl"),
    )
    return jax.shard_map(
        on_device, mesh=mesh, in_specs=in_specs, out_specs=out_specs, check_vma=False
    )
```

profile of v0, /device:TPU:8, one launch (start us, length us, event | category | flops | bytes accessed | tf_op | source)
XLA Modules:
  0.0 1558.7 jit_solution(11045563871013030518)
XLA Ops:
  7.2 0.0 copy-start
  7.2 0.0 copy-start.5
  7.2 0.0 all-gather.7.cloned.1.call-start
  7.2 0.7 all-gather.7.cloned.1.call-update
  7.9 0.0 all-gather.5.cloned.1.call-start
  8.0 1.9 collective-permute-start
  9.9 1.4 collective-permute-done
  11.3 0.0 copy-start.6
  11.3 0.6 copy-done.6
  11.9 0.0 all-gather.5.cloned.1.call-update
  11.9 0.0 all-reduce.5.cloned.1.call-start
  12.0 362.7 %all-gather.1 = s32[128,8,4]{1,2,0:T(4,128)S(1)} all-gather(s32[1,8,4]{1,2,0:T(4,128)} %bitcast.76), channel_id=1, replica_groups=mesh['tower'=2,'blk'=128,'mdl'=2] {'blk'}, dimensions={0}, use_global_device_ids=true | all-gather | bytes 16512 | tf_op jit(solution)/shard_map/all_gather | solution.py:61
  374.7 0.2 reshape.99
  374.9 0.7 convert_element_type.34
  375.5 1.3 dynamic-slice
  377.4 0.9 dynamic-update-slice.1
  378.3 23.6 %all-reduce.1 = s32[1024]{0:T(1024)S(1)} all-reduce(s32[1024]{0:T(1024)S(1)} %dynamic-update-slice.1), channel_id=1, replica_groups=mesh['tower'=2,'blk'=128,'mdl'=2] {'blk'}, use_global_device_ids=true, to_apply=%add.1 | all-reduce | flops 1024 | bytes 8192
  401.9 0.7 iota_compare_fusion.2
  402.6 0.8 select_reduce_fusion.1
  403.4 0.1 select_reduce_fusion
  403.5 0.0 copy-start.2
  403.5 0.0 all-gather.7.cloned.1.call-done
  403.5 0.0 copy-done
  403.5 4.5 fusion.6
  408.0 51.9 %all-gather.5.cloned.1.call-done = bf16[1024,2048]{1,0:T(8,128)(2,1)} async-done(((bf16[8,2048]{1,0:T(8,128)(2,1)}), bf16[1024,2048]{1,0:T(8,128)(2,1)}) %all-gather.5.cloned.1.call-update) | async-done | bytes 4194320 | tf_op jit(solution)/shard_map/all_gather | solution.py:53
  459.9 0.0 copy-done.5
  459.9 3.4 fusion.44
  463.3 8.4 psum.35
  471.6 0.1 multiply_reduce_fusion
  471.8 0.2 exponential_reduce_fusion
  472.0 0.1 fusion.49
  472.1 355.2 %all-reduce = f32[1024]{0:T(1024)S(1)} all-reduce(f32[1024]{0:T(1024)S(1)} %get-tuple-element.6), channel_id=1, replica_groups=mesh['tower'=2,'blk'=128,'mdl'=2] {'blk'}, use_global_device_ids=true, to_apply=%add | all-reduce | flops 1024 | bytes 8192
  827.3 0.0 copy-start.3
  827.3 1.4 collective-permute-start.1
  828.7 0.0 copy-done.2
  828.7 4.4 fusion.4
  833.2 0.0 all-reduce.5.cloned.1.call-update
  833.2 0.0 collective-permute-done.1
  833.2 2.9 fusion.33
  836.1 700.7 %psum.36 = bf16[8,2048]{1,0:T(8,128)(2,1)S(1)} all-reduce(bf16[8,2048]{1,0:T(8,128)(2,1)S(1)} %get-tuple-element.8), channel_id=1, replica_groups=mesh['tower'=2,'blk'=128,'mdl'=2] {'blk'}, use_global_device_ids=true, to_apply=%region_5.6 | all-reduce | flops 16384 | bytes 65536 | tf_op jit(solution)/shard_map/psum | solution.py:32
  1536.8 0.0 copy-done.3
  1536.8 0.2 convolution_bitcast_fusion
  1537.0 5.6 psum.37
  1542.7 0.1 copy.22
  1542.8 0.6 multiply_bitcast_fusion
  1543.4 0.0 all-reduce.5.cloned.1.call-done
  1543.4 1.3 convert_bitcast_fusion
  1544.7 0.0 copy-start.4
  1544.7 0.1 copy.24
  1544.8 0.2 reduce_sum.39
  1545.0 0.0 copy-start.1
  1545.0 1.3 fusion.14
  1546.3 0.2 broadcast_in_dim.74
  1546.4 4.1 fusion.18
  1550.5 0.0 copy-done.4
  1550.5 0.0 copy-done.1
  1550.5 1.6 fusion.15
  (6 shorter events, 0.0 us)
Async XLA Ops:
  7.2 396.3 %copy-start = (bf16[1,112,2048]{2,1,0:T(8,128)(2,1)S(1)}, bf16[1,112,2048]{2,1,0:T(8,128)(2,1)}, u32[]{:S(2)}) copy-start(bf16[1,112,2048]{2,1,0:T(8,128)(2,1)} %param.12) | copy-start | bytes 1376260
  7.2 452.7 %copy-start.5 = (bf16[1,8,2048]{2,1,0:T(8,128)(2,1)S(1)}, bf16[1,8,2048]{2,1,0:T(8,128)(2,1)}, u32[]{:S(2)}) copy-start(bf16[1,8,2048]{2,1,0:T(8,128)(2,1)} %param.7) | copy-start | bytes 98308
  7.2 396.3 %all-gather.7.cloned.1.call-start = ((), (), s32[]{:S(2)}) async-start(), calls=%async_computation.1 | async-start | bytes 4227072 | tf_op jit(solution)/shard_map/all_gather | solution.py:74
  7.9 452.0 %all-gather.5.cloned.1.call-start = ((), (), s32[]{:S(2)}) async-start(), calls=%async_computation | async-start | bytes 4227072 | tf_op jit(solution)/shard_map/all_gather | solution.py:53
  8.0 3.3 collective-permute-start
  11.3 0.6 copy-start.6
  11.9 1531.5 %all-reduce.5.cloned.1.call-start = ((), (), s32[]{:S(2)}) async-start(), calls=%async_computation.2 | async-start | bytes 1835008 | tf_op jit(solution)/shard_map/psum | solution.py:82
  403.5 425.2 %copy-start.2 = (bf16[1,112,2048]{2,1,0:T(8,128)(2,1)S(1)}, bf16[1,112,2048]{2,1,0:T(8,128)(2,1)}, u32[]{:S(2)}) copy-start(bf16[1,112,2048]{2,1,0:T(8,128)(2,1)} %param.11) | copy-start | bytes 1376260
  827.3 709.5 %copy-start.3 = (bf16[1,112,2048]{2,1,0:T(8,128)(2,1)S(1)}, bf16[1,112,2048]{2,1,0:T(8,128)(2,1)}, u32[]{:S(2)}) copy-start(bf16[1,112,2048]{2,1,0:T(8,128)(2,1)} %param.13) | copy-start | bytes 1376260
  827.3 5.9 collective-permute-start.1
  1544.7 5.9 copy-start.4
  1545.0 5.6 copy-start.1
Sparse Core Ops, SparseCore 0:
  12.6 225.5 all-gather.6
  243.4 216.4 all-gather.4
  833.3 46.1 all-reduce.4
where the time goes:
time: 1560 us
  blocking collectives  1460 us (94%)
  waiting for transfers between devices  54 us (3%)
  matrix products  22.4 us (1%)
    psum x1, blocking collectives, broadcast(): return lax.psum(block, axis)  701 us
    unnamed x2, blocking collectives  379 us
    all_gather x1, blocking collectives, on_device(): lax.all_gather(pos_index, 'blk', axis=0, tiled=True)  363 us
    all_gather x1, waiting for transfers between devices, on_device(): others = lax.all_gather(partner, 'blk', axis=0, tiled=True)  51.9 us
  transfers between devices with their start and end apart: 5, of which 2 were waited for; matrix products, arithmetic and copies ran while one was open for 1% of the time, Pallas kernels for 0%

commit v1 on v0

v1 whole, which is shorter than its diff:
```python
import functools

import jax
import jax.numpy as jnp
from jax import lax
from jax.experimental import pallas as pl
from jax.experimental.pallas import tpu as pltpu
from jax.sharding import PartitionSpec as P

D = 4096
SEQ = 128
KPOS = 4
LOSS_SCALE = 256.0
SCORE_SCALE = D ** (-0.5)
GRAD_SCALE = LOSS_SCALE * SCORE_SCALE

F32 = jnp.float32
BF16 = jnp.bfloat16
NT = (((1,), (1,)), ((), ()))
TN = (((0,), (0,)), ((), ()))
NN = (((1,), (0,)), ((), ()))

W = 2048
EXT = W + 128
U = 112
NX, NYH, NZ, NZL = 4, 2, 16, 4
NG, NP = 16, 8


def dot(a, b, dims):
    return lax.dot_general(a, b, dims, preferred_element_type=F32)


def slot_right(distance):
    return 0 if distance == 0 else (15 if distance == 8 else 2 * distance - 1)


def slot_left(distance):
    return 0 if distance == 0 else (15 if distance == 8 else 2 * distance)


def thirds(value):
    a = value.astype(BF16)
    rest = value - a.astype(F32)
    b = rest.astype(BF16)
    c = (rest - b.astype(F32)).astype(BF16)
    return a, b, c


def kernel(
    emb_ref, tok_ref, wg_ref, wu_ref, wd_ref,
    eg_ref, gg_ref, gu_ref, gd_ref,
    gb, pb, tok, s_own, s_in, stats, go, rs1, r2, rs2, mbp, mbr, mb, mbp1, mbr1,
    bk_own, bk_in, gown, gsend, gin, act1, act2, pool, grads,
    e1_s, e1_r, e2_s, e2_r, fw_s, fw_r, m1_s, m1_r, l1_s, l1_r, r1_s, r1_r, r2_s, r2_r,
    mq_s, mq_r, mp_s, mp_r, ma_s, ma_r, d_s, d_r, t1_s, t1_r, t2_s, t2_r,
    zr_s, zr_r, zl_s, zl_r, gu_s, gu_r,
):
    t = lax.axis_index("tower")
    b = lax.axis_index("blk")
    m = lax.axis_index("mdl")
    x = b // 32
    yh = (b // 16) % 2
    z = b % 16
    zh = z // 4
    zl = z % 4
    xy = b // 16
    gslot = x * NZL + zl
    pslot = yh * 4 + zh

    def blk_of(x_, yh_, zh_, zl_):
        return (x_ * 2 + yh_) * 16 + zh_ * 4 + zl_

    def goal_peer(k):
        q = (gslot + k) % NG
        return blk_of(q // 4, yh, zh, q % 4)

    def premise_peer(k):
        q = (pslot + k) % NP
        return blk_of(x, q // 4, q % 4, zl)

    def copy(src, dst, ss, rs, dev):
        return pltpu.make_async_remote_copy(
            src_ref=src, dst_ref=dst, send_sem=ss, recv_sem=rs,
            device_id=dev, device_id_type=pl.DeviceIdType.MESH,
        )

    def each_role(f):
        for role in (0, 1):
            @pl.when(t == role)
            def _(role=role):
                f(role)

    barrier = pltpu.get_barrier_semaphore()
    everyone = [{"blk": goal_peer(k)} for k in range(1, NG)]
    everyone += [{"blk": premise_peer(k)} for k in range(1, NP)]
    everyone += [{"blk": xy * 16 + (z + 1) % 16}, {"blk": xy * 16 + (z + 15) % 16}]
    everyone += [{"mdl": 1 - m}, {"tower": 1 - t}]
    for dev in everyone:
        pl.semaphore_signal(barrier, inc=1, device_id=dev, device_id_type=pl.DeviceIdType.MESH)
    pl.semaphore_wait(barrier, len(everyone))

    def role_of(role):
        if role == 0:
            return gb, NX, x, zl, (lambda k: blk_of((x + k) % NX, yh, zh, zl)), (
                lambda k: blk_of(x, yh, zh, (zl + k) % 4))
        return pb, NYH, yh, zh, (lambda k: blk_of(x, (yh + k) % NYH, zh, zl)), (
            lambda k: blk_of(x, yh, (zh + k) % 4, zl))

    def e1_copy(role, k):
        buf, _, mo, mi, _, inner = role_of(role)
        return copy(emb_ref, buf.at[mo * 4 + mi], e1_s.at[k - 1], e1_r.at[k - 1], {"blk": inner(k)})

    def e1_arrival(role, k):
        buf, _, mo, mi, _, inner = role_of(role)
        return copy(emb_ref, buf.at[mo * 4 + (mi - k + 4) % 4], e1_s.at[k - 1], e1_r.at[k - 1], {"blk": inner(k)})

    def e2_copy(role, k, back=0):
        buf, no, mo, _, outer, _ = role_of(role)
        part = buf.at[pl.ds(((mo - back + no) % no) * 4, 4)]
        return copy(part, part, e2_s.at[k - 1], e2_r.at[k - 1], {"blk": outer(k)})

    def fw_copy(role, k):
        buf, no, mo, _, _, _ = role_of(role)
        part = buf.at[pl.ds(((mo - k + no) % no) * 4, 4)]
        return copy(part, part, fw_s.at[k], fw_r.at[k], {"tower": 1 - t})

    def start_e1(role):
        buf, _, mo, mi, _, _ = role_of(role)
        buf[mo * 4 + mi] = emb_ref[...]
        for k in range(1, 4):
            e1_copy(role, k).start()

    each_role(start_e1)

    tok[0, xy] = tok_ref[...]

    def t1_copy(row):
        return copy(tok_ref, tok.at[0, row], t1_s.at[0], t1_r.at[0], {"blk": blk_of(x, 1 - yh, zh, zl)})

    def t2_copy(k, back=0):
        part = tok.at[0, pl.ds(((x - back + NX) % NX) * 2, 2)]
        return copy(part, part, t2_s.at[k - 1], t2_r.at[k - 1], {"blk": blk_of((x + k) % NX, yh, zh, zl)})

    def ring_copy(step, half, right):
        slot = slot_right if right else slot_left
        rows = pl.ds(4 * half, 4)
        ss, rs = (zr_s, zr_r) if right else (zl_s, zl_r)
        nxt = (z + 1) % 16 if right else (z + 15) % 16
        return copy(
            tok.at[slot(step - 1), rows], tok.at[slot(step), rows],
            ss.at[step - 1, half], rs.at[step - 1, half], {"blk": xy * 16 + nxt},
        )

    def ring_parts(step):
        for half in (0, 1):
            for right in (True, False):
                if step < 8 or (half == 0) == right:
                    yield half, right

    def ring_start(step):
        for half, right in ring_parts(step):
            ring_copy(step, half, right).start()

    def ring_step(step):
        nxt = set(ring_parts(step + 1)) if step < 8 else set()
        for half, right in ring_parts(step):
            ring_copy(step, half, right).wait_recv()
            if (half, right) in nxt:
                ring_copy(step + 1, half, right).start()

    t1_copy(xy).start()
    t1_copy(x * 2 + 1 - yh).wait_recv()
    for k in range(1, NX):
        t2_copy(k).start()

    def start_e2(role):
        for k in range(1, 4):
            e1_arrival(role, k).wait_recv()
        for k in range(1, role_of(role)[1]):
            e2_copy(role, k).start()
        fw_copy(role, 0).start()

    each_role(start_e2)

    for k in range(1, NX):
        t2_copy(k, back=k).wait_recv()
    ring_start(1)

    def forward(role):
        for k in range(1, role_of(role)[1]):
            e2_copy(role, k, back=k).wait_recv()
            fw_copy(role, k).start()
        for k in range(role_of(1 - role)[1]):
            fw_copy(1 - role, k).wait_recv()

    each_role(forward)

    goals = gb[:, :, :W].reshape(NG * 8, W)
    premises = pb[:, :, :W].reshape(NP * 8, W)
    s_own[...] = dot(premises, goals, NT)
    m1 = copy(s_own, s_in, m1_s.at[0], m1_r.at[0], {"mdl": 1 - m})
    m1.start()

    codes = jnp.transpose(gb[:, :, W:].astype(F32).reshape(NG * 8, 128))
    count = codes[8:9]
    row = lax.broadcasted_iota(jnp.int32, (NP * 8, NG * 8), 0)
    member = row // 8
    premise_id = (blk_of(x, member // 4, member % 4, zl) * 8 + row % 8).astype(F32)
    weights = jnp.zeros((NP * 8, NG * 8), F32)
    for k in range(KPOS):
        listed = codes[k:k + 1] * 32.0 + codes[4 + k:5 + k]
        hit = (listed == premise_id) & (count > float(k))
        weights = weights + jnp.where(hit, 1.0, 0.0)
    weights = weights / count

    ring_step(1)
    m1.wait_recv()
    scores = (s_own[...] + s_in[...]) * SCORE_SCALE
    top = jnp.max(scores, axis=0, keepdims=True)
    total = jnp.sum(jnp.exp(scores - top), axis=0, keepdims=True)
    stats[0] = jnp.concatenate([top, total, jnp.zeros((6, 128), F32)], axis=0)

    def l1_copy(k):
        return copy(stats.at[0], stats.at[k], l1_s.at[k - 1], l1_r.at[k - 1], {"blk": goal_peer(k)})

    for k in range(1, NG):
        l1_copy(k).start()

    def gate_copy(c):
        return copy(gsend.at[c], gin.at[c], gu_s.at[c], gu_r.at[c], {"mdl": 1 - m})

    def gate_chunk(c):
        rows = tok[4 * c:4 * c + 4].reshape(256, W)
        g = dot(wg_ref[...], rows, NT)
        u = dot(wu_ref[...], rows, NT)
        gown[c, :U] = g
        gown[c, U:] = u
        gsend[c, :U] = g.astype(BF16)
        gsend[c, U:] = u.astype(BF16)
        gate_copy(c).start()

    def spread(dtype):
        lane = lax.broadcasted_iota(jnp.int32, (8, 256), 1)
        sub = lax.broadcasted_iota(jnp.int32, (8, 256), 0)
        return jnp.where((lane // 8) % 8 == sub, 1.0, 0.0).astype(dtype)

    def act_chunk(c):
        gate_copy(c).wait_recv()
        g = gown[c, :U] + gin[c, :U].astype(F32)
        u = gown[c, U:] + gin[c, U:].astype(F32)
        s = 1.0 / (1.0 + jnp.exp(-g))
        a = g * s
        hidden = (a * u).astype(BF16)
        act1[c] = u * (s * (1.0 + g * (1.0 - s)))
        act2[c] = a
        part = dot(spread(BF16), hidden, NT)
        if c == 0:
            pool[:, :U] = part
        else:
            pool[:, :U] += part

    ring_step(2)
    gate_chunk(0)

    for k in range(1, NG):
        l1_copy(k).wait_recv()
    tops = [stats[k, 0:1] for k in range(NG)]
    peak = functools.reduce(jnp.maximum, tops)
    mass = functools.reduce(lambda p, q: p + q, [stats[k, 1:2] * jnp.exp(tops[k] - peak) for k in range(NG)])
    lse = peak + jnp.log(mass)
    coefficient = jnp.exp(scores - lse) - weights

    def mq_copy(role, k):
        if role == 0:
            return copy(mbp.at[(gslot + k) % NG], mbr.at[k - 1], mq_s.at[k - 1], mq_r.at[k - 1], {"blk": goal_peer(k)})
        return copy(mbp1.at[(pslot + k) % NP], mbr1.at[k - 1], mq_s.at[k - 1], mq_r.at[k - 1], {"blk": premise_peer(k)})

    def r1_copy(role, k):
        _, no, mo, _, outer, _ = role_of(role)
        return copy(go.at[pl.ds(((mo + k) % no) * 4, 4)], rs1.at[k - 1], r1_s.at[k - 1], r1_r.at[k - 1], {"blk": outer(k)})

    def r2_copy(role, k):
        _, _, _, mi, _, inner = role_of(role)
        return copy(r2.at[(mi + k) % 4], rs2.at[k - 1], r2_s.at[k - 1], r2_r.at[k - 1], {"blk": inner(k)})

    def in_first(role):
        return (pslot if role == 0 else gslot) == 0

    def members(role):
        return NG if role == 0 else NP

    def start_sums(role):
        if role == 0:
            lhs = jnp.transpose(coefficient).astype(BF16)
            other = premises
        else:
            lhs = coefficient.astype(BF16)
            other = goals
        part = dot(lhs, other, NN)
        n = members(role)
        wide = W // n
        go[:n] = part.astype(BF16).reshape(n, 8, W)

        @pl.when(in_first(role))
        def _():
            target = mbp if role == 0 else mbp1
            for q in range(n):
                target[q] = part[:8, q * wide:(q + 1) * wide]
            for k in range(1, n):
                mq_copy(role, k).start()

        for k in range(1, role_of(role)[1]):
            r1_copy(role, k).start()

    each_role(start_sums)
    ring_step(3)

    def slice_of(role, q):
        wide = W // members(role)
        return mb.at[:, pl.ds(pl.multiple_of(q * wide, wide), wide)]

    def mp_copy(role, k):
        part = slice_of(role, gslot if role == 0 else pslot)
        return copy(part, part, mp_s.at[k - 1], mp_r.at[0],
                    {"blk": premise_peer(k) if role == 0 else goal_peer(k)})

    def ma_copy(role, k, back=0):
        n = members(role)
        me = gslot if role == 0 else pslot
        part = slice_of(role, (me - back + n) % n)
        return copy(part, part, ma_s.at[k - 1], ma_r.at[k - 1],
                    {"blk": goal_peer(k) if role == 0 else premise_peer(k)})

    def spread_micro(role):
        n = members(role)
        wide = W // n
        me = gslot if role == 0 else pslot
        own, got = (mbp, mbr) if role == 0 else (mbp1, mbr1)

        @pl.when(in_first(role))
        def _():
            acc = own[me]
            for k in range(1, n):
                mq_copy(role, k).wait_recv()
                acc = acc + got[k - 1]
            lo = pl.multiple_of(me * wide, wide)
            mb[:, pl.ds(lo, wide)] = ((GRAD_SCALE * acc) / SEQ).astype(BF16)
            for k in range(1, members(1 - role)):
                mp_copy(role, k).start()

        @pl.when(jnp.logical_not(in_first(role)))
        def _():
            mp_copy(role, 1).wait_recv()

        for k in range(1, n):
            ma_copy(role, k).start()

    each_role(spread_micro)

    def second_sums(role):
        _, no, mo, _, _, _ = role_of(role)
        acc = go[pl.ds(mo * 4, 4)].astype(F32)
        for k in range(1, no):
            r1_copy(role, k).wait_recv()
            acc = acc + rs1[k - 1].astype(F32)
        r2[...] = acc.astype(BF16)
        for k in range(1, 4):
            r2_copy(role, k).start()

    each_role(second_sums)
    ring_step(4)
    gate_chunk(1)

    def all_micro(role):
        for k in range(1, members(role)):
            ma_copy(role, k, back=k).wait_recv()

    each_role(all_micro)
    bk_own[:, :U] = dot(mb[...], wd_ref[...], NT)
    bk_own[:, U:] = jnp.zeros((8, 128 - U), F32)
    back = copy(bk_own, bk_in, d_s.at[0], d_r.at[0], {"mdl": 1 - m})
    back.start()
    ring_step(5)

    def last_sums(role):
        mi = role_of(role)[3]
        acc = r2[mi].astype(F32)
        for k in range(1, 4):
            r2_copy(role, k).wait_recv()
            acc = acc + rs2[k - 1].astype(F32)
        eg_ref[...] = GRAD_SCALE * acc

    each_role(last_sums)
    act_chunk(0)
    ring_step(6)
    gate_chunk(2)
    act_chunk(1)
    back.wait_recv()
    back_rows = jnp.transpose(bk_own[...] + bk_in[...])[:U]

    def back_chunk(c):
        wide = sum(dot(p, spread(BF16), NN) for p in thirds(back_rows))
        grads[:U, 256 * c:256 * c + 256] = (wide * act1[c]).astype(BF16)
        grads[U:, 256 * c:256 * c + 256] = (wide * act2[c]).astype(BF16)

    ring_step(7)
    act_chunk(2)
    for c in range(3):
        back_chunk(c)
    ring_step(8)
    gate_chunk(3)
    act_chunk(3)
    back_chunk(3)

    pool[:, U:] = jnp.zeros((8, 128 - U), F32)
    pooled = thirds(jnp.transpose(pool[...])[:U])
    gd_ref[...] = sum(dot(p, mb[...], NN) for p in pooled).astype(BF16)

    @pl.loop(0, W // 512)
    def _(j):
        cols = pl.ds(pl.multiple_of(j * 512, 512), 512)
        both = dot(grads[...], tok[:, :, :, cols].reshape(1024, 512), NN)
        gg_ref[:, cols] = both[:U].astype(BF16)
        gu_ref[:, cols] = both[U:].astype(BF16)

    def drain(role):
        n = members(role)
        for k in range(1, 4):
            e1_copy(role, k).wait_send()
            r2_copy(role, k).wait_send()
        for k in range(1, role_of(role)[1]):
            e2_copy(role, k).wait_send()
            r1_copy(role, k).wait_send()
        for k in range(role_of(role)[1]):
            fw_copy(role, k).wait_send()
        for k in range(1, n):
            ma_copy(role, k).wait_send()

        @pl.when(in_first(role))
        def _():
            for k in range(1, n):
                mq_copy(role, k).wait_send()
            for k in range(1, members(1 - role)):
                mp_copy(role, k).wait_send()

    each_role(drain)
    t1_copy(xy).wait_send()
    for k in range(1, NX):
        t2_copy(k).wait_send()
    for step in range(1, 9):
        for half, right in ring_parts(step):
            ring_copy(step, half, right).wait_send()
    m1.wait_send()
    back.wait_send()
    for k in range(1, NG):
        l1_copy(k).wait_send()
    for c in range(4):
        gate_copy(c).wait_send()


def on_device(embeddings, pos_index, pos_count, hidden_in, w_gate, w_up, w_down):
    coded = jnp.concatenate([pos_index // 32, pos_index % 32, pos_count[:, None]], axis=1)
    coded = jnp.pad(coded.astype(BF16), ((0, 0), (0, 128 - coded.shape[1])))
    own = jnp.concatenate([embeddings[0], coded], axis=1)
    vmem = pl.BlockSpec(memory_space=pltpu.VMEM)
    dma = pltpu.SemaphoreType.DMA
    counts = [3, 3, 3, 3, 4, 4, 1, 1, 15, 15, 3, 3, 3, 3, 15, 15, 15, 1, 15, 15, 1, 1, 1, 1, 3, 3]
    out = pl.pallas_call(
        kernel,
        out_shape=(
            jax.ShapeDtypeStruct((8, W), F32),
            jax.ShapeDtypeStruct((U, W), BF16),
            jax.ShapeDtypeStruct((U, W), BF16),
            jax.ShapeDtypeStruct((U, W), BF16),
        ),
        in_specs=[vmem] * 5,
        out_specs=(vmem,) * 4,
        scratch_shapes=[
            pltpu.VMEM((NG, 8, EXT), BF16),
            pltpu.VMEM((NP, 8, EXT), BF16),
            pltpu.VMEM((NZ, 8, 8, W), BF16),
            pltpu.VMEM((NP * 8, NG * 8), F32),
            pltpu.VMEM((NP * 8, NG * 8), F32),
            pltpu.VMEM((NG, 8, 128), F32),
            pltpu.VMEM((NG, 8, W), BF16),
            pltpu.VMEM((3, 4, 8, W), BF16),
            pltpu.VMEM((4, 8, W), BF16),
            pltpu.VMEM((3, 8, W), BF16),
            pltpu.VMEM((NG, 8, 128), F32),
            pltpu.VMEM((NG - 1, 8, 128), F32),
            pltpu.VMEM((8, W), BF16),
            pltpu.VMEM((NP, 8, 256), F32),
            pltpu.VMEM((NP - 1, 8, 256), F32),
            pltpu.VMEM((8, 128), F32),
            pltpu.VMEM((8, 128), F32),
            pltpu.VMEM((4, 2 * U, 256), F32),
            pltpu.VMEM((4, 2 * U, 256), BF16),
            pltpu.VMEM((4, 2 * U, 256), BF16),
            pltpu.VMEM((4, U, 256), F32),
            pltpu.VMEM((4, U, 256), F32),
            pltpu.VMEM((8, 128), F32),
            pltpu.VMEM((2 * U, 1024), BF16),
        ]
        + [dma((n,)) for n in counts]
        + [dma((8, 2))] * 4
        + [dma((4,))] * 2,
        compiler_params=pltpu.CompilerParams(
            collective_id=0, has_side_effects=True, vmem_limit_bytes=48 * 1024 * 1024
        ),
    )(own, hidden_in[0], w_gate[0], w_up[0], w_down[0])
    return tuple(v[None] for v in out)


def solution(mesh):
    wide = P("tower", "blk", "mdl")
    return jax.shard_map(
        on_device,
        mesh=mesh,
        in_specs=(wide, P("blk", None), P("blk"), wide, wide, wide, wide),
        out_specs=(wide,) * 4,
        check_vma=False,
    )
```

time: 1560 us -> 99.1 us (0.06)
  the two profiles are of different devices: /device:TPU:8 before, /device:TPU:18 now
where the time goes in v1:
time: 99.1 us; the launch traced here: 98.7 us
  Pallas kernels  89.7 us (91%)
  local copies, waits for them, and re-layouts  7.59 us (8%)
    pallas_call x1, Pallas kernels, on_device(): pl.pallas_call(kernel, out_shape=(jax.ShapeDtypeStruct((8, W), F32), jax....  89.7 us
    unnamed x15, local copies, waits for them, and re-layouts  7.5 us

profile of v1, /device:TPU:18, one launch (start us, length us, event | category | flops | bytes accessed | tf_op | source)
XLA Modules:
  0.0 98.7 jit_solution(10619767004743305891)
XLA Ops:
  0.6 0.0 copy-start.4
  0.6 0.7 convert_bitcast_fusion
  1.3 0.1 copy.15
  1.4 0.8 copy.11
  2.2 0.1 fusion.8
  2.3 0.0 copy-done.4
  2.3 0.0 copy-start.3
  2.3 0.8 copy-done.3
  3.0 0.0 copy-start
  3.0 1.0 %copy-done = bf16[1,112,2048]{2,1,0:T(8,128)(2,1)S(1)} copy-done((bf16[1,112,2048]{2,1,0:T(8,128)(2,1)S(1)}, bf16[1,112,2048]{2,1,0:T(8,128)(2,1)}, u32[]{:S(2)}) %copy-start) | copy-done | bytes 458776
  4.0 0.0 copy-start.1
  4.0 1.0 %copy-done.1 = bf16[1,112,2048]{2,1,0:T(8,128)(2,1)S(1)} copy-done((bf16[1,112,2048]{2,1,0:T(8,128)(2,1)S(1)}, bf16[1,112,2048]{2,1,0:T(8,128)(2,1)}, u32[]{:S(2)}) %copy-start.1) | copy-done | bytes 458776
  5.1 0.0 copy-start.2
  5.1 1.0 %copy-done.2 = bf16[1,112,2048]{2,1,0:T(8,128)(2,1)S(1)} copy-done((bf16[1,112,2048]{2,1,0:T(8,128)(2,1)S(1)}, bf16[1,112,2048]{2,1,0:T(8,128)(2,1)}, u32[]{:S(2)}) %copy-start.2) | copy-done | bytes 458776
  6.1 89.7 %shard_map.102 = (f32[8,2048]{1,0:T(8,128)S(1)}, bf16[112,2048]{1,0:T(8,128)(2,1)S(1)}, bf16[112,2048]{1,0:T(8,128)(2,1)S(1)}, bf16[112,2048]{1,0:T(8,128)(2,1)S(1)}) custom-call(bf16[8,2176]{1,0:T(8,128)(2,1)S(1)} %pad_maximum_fusion.emb_ref, bf16[8,2048]{1,0:T(8,128)(2,1)S(1)} %bitcast.18, bf16[112,2048]{1,0:T(8,128)(2,1)S(1)} %bitcast.14, ...), custom_call_target="tpu_custom_call" | custom-call | tf_op jit(solution)/shard_map/pallas_call | solution.py:469
  95.8 0.6 copy.20
  96.4 0.8 copy.21
  97.2 0.8 copy.22
  97.9 0.8 copy.23
  (2 shorter events, 0.0 us)
Async XLA Ops:
  0.6 1.6 %copy-start.4 = (bf16[1,8,2048]{2,1,0:T(8,128)(2,1)S(1)}, bf16[1,8,2048]{2,1,0:T(8,128)(2,1)}, u32[]{:S(2)}) copy-start(bf16[1,8,2048]{2,1,0:T(8,128)(2,1)} %param.7) | copy-start | bytes 98308
  2.3 0.8 copy-start.3
  3.0 1.0 %copy-start = (bf16[1,112,2048]{2,1,0:T(8,128)(2,1)S(1)}, bf16[1,112,2048]{2,1,0:T(8,128)(2,1)}, u32[]{:S(2)}) copy-start(bf16[1,112,2048]{2,1,0:T(8,128)(2,1)} %param.11) | copy-start | bytes 1376260
  4.0 1.0 %copy-start.1 = (bf16[1,112,2048]{2,1,0:T(8,128)(2,1)S(1)}, bf16[1,112,2048]{2,1,0:T(8,128)(2,1)}, u32[]{:S(2)}) copy-start(bf16[1,112,2048]{2,1,0:T(8,128)(2,1)} %param.12) | copy-start | bytes 1376260
  5.1 1.0 %copy-start.2 = (bf16[1,112,2048]{2,1,0:T(8,128)(2,1)S(1)}, bf16[1,112,2048]{2,1,0:T(8,128)(2,1)}, u32[]{:S(2)}) copy-start(bf16[1,112,2048]{2,1,0:T(8,128)(2,1)} %param.13) | copy-start | bytes 1376260

commit v2 on v1

v2 whole, which is shorter than its diff:
```python
import functools

import jax
import jax.numpy as jnp
from jax import lax
from jax.experimental import pallas as pl
from jax.experimental.pallas import tpu as pltpu
from jax.sharding import PartitionSpec as P

D = 4096
SEQ = 128
KPOS = 4
LOSS_SCALE = 256.0
SCORE_SCALE = D ** (-0.5)
GRAD_SCALE = LOSS_SCALE * SCORE_SCALE

F32 = jnp.float32
BF16 = jnp.bfloat16
NT = (((1,), (1,)), ((), ()))
NN = (((1,), (0,)), ((), ()))

W = 2048
FIRST, SECOND, THIRD = pl.ds(0, 1024), pl.ds(1024, 512), pl.ds(1536, 512)
FIRST_SECOND = pl.ds(0, 1536)
TILE = 512
U = 112
NX, NYH, NZ = 4, 2, 16
NG, NP = 16, 8


def dot(a, b, dims):
    return lax.dot_general(a, b, dims, preferred_element_type=F32)


def thirds(value):
    a = value.astype(BF16)
    rest = value - a.astype(F32)
    b = rest.astype(BF16)
    c = (rest - b.astype(F32)).astype(BF16)
    return a, b, c


def kernel(
    pos_ref, cnt_ref, emb_ref, hid_ref, wg_hbm, wu_hbm, wd_hbm,
    eg_ref, gg_ref, gu_ref, gd_ref,
    mb, pool, grads, tok, early,
    gb, pb, wg_ref, wu_ref, wd_ref, s_own, s_in, stats, go, rs1, r2, rs2, mbp, mbr, mbp1, mbr1,
    bk_own, bk_in, gown, gsend, gin, act1, act2,
    loc, e1_s, e1_r, e2_s, e2_r, fw_s, fw_r, m1_s, m1_r, l1_s, l1_r, r1_s, r1_r, r2_s, r2_r,
    mq_s, mq_r, mp_s, mp_r, ma_s, ma_r, d_s, d_r,
    za_s, za_r, zb_s, zb_r, yb_s, yb_r, xb_s, xb_r, yc_s, yc_r, xc_s, xc_r, yd_s, yd_r, xd_s, xd_r, zd_s, zd_r, gu_s, gu_r,
):
    t = lax.axis_index("tower")
    b = lax.axis_index("blk")
    m = lax.axis_index("mdl")
    xy = lax.div(b, 16)
    z = lax.rem(b, 16)
    x = lax.div(xy, 2)
    yh = lax.rem(xy, 2)
    zh = lax.div(z, 4)
    zl = lax.rem(z, 4)
    gslot = x * 4 + zl
    pslot = yh * 4 + zh

    def blk_of(x_, yh_, zh_, zl_):
        return (x_ * 2 + yh_) * 16 + zh_ * 4 + zl_

    x_at = [x] + [lax.rem(x + k, 4) for k in (1, 2, 3)]
    zl_at = [zl] + [lax.rem(zl + k, 4) for k in (1, 2, 3)]
    zh_at = [zh] + [lax.rem(zh + k, 4) for k in (1, 2, 3)]
    yh_at = [yh, 1 - yh]

    goal_ids = [blk_of(x_at[k // 4], yh, zh, zl_at[k % 4]) for k in range(NG)]
    premise_ids = [blk_of(x, yh_at[k // 4], zh_at[k % 4], zl) for k in range(NP)]
    z_ids = {d: xy * 16 + lax.rem(z + d + 16, 16) for d in (1, -1, 2, -2)}
    y_id = premise_ids[4]
    x_ids = [goal_ids[4 * k] for k in range(NX)]

    def goal_slot(k, back=False):
        o, i = k // 4, k % 4
        return x_at[(4 - o) % 4 if back else o] * 4 + zl_at[(4 - i) % 4 if back else i]

    def premise_slot(k, back=False):
        o, i = k // 4, k % 4
        return yh_at[o] * 4 + zh_at[(4 - i) % 4 if back else i]

    def copy(src, dst, ss, rs, dev):
        return pltpu.make_async_remote_copy(
            src_ref=src, dst_ref=dst, send_sem=ss, recv_sem=rs,
            device_id=dev, device_id_type=pl.DeviceIdType.MESH,
        )

    def each_role(f):
        for role in (0, 1):
            @pl.when(t == role)
            def _(role=role):
                f(role)

    def count_of(role):
        return (NG, NP)[role]

    def ids_of(role):
        return (goal_ids, premise_ids)[role]

    def slot_of(role, k, back=False):
        return (goal_slot, premise_slot)[role](k, back)

    barrier = pltpu.get_barrier_semaphore()
    everyone = [{"blk": v} for v in goal_ids[1:] + premise_ids[1:] + list(z_ids.values())]
    everyone += [{"mdl": 1 - m}, {"tower": 1 - t}]
    for dev in everyone:
        pl.semaphore_signal(barrier, inc=1, device_id=dev, device_id_type=pl.DeviceIdType.MESH)

    def own_emb(role):
        return pltpu.make_async_copy(emb_ref.at[0], (gb, pb)[role].at[slot_of(role, 0)], loc.at[0])

    own_tok = pltpu.make_async_copy(hid_ref.at[0], tok.at[0, x, yh], loc.at[1])
    own_wg = pltpu.make_async_copy(wg_hbm.at[0], wg_ref, loc.at[2])
    own_wu = pltpu.make_async_copy(wu_hbm.at[0], wu_ref, loc.at[3])
    own_wd = pltpu.make_async_copy(wd_hbm.at[0], wd_ref, loc.at[4])
    each_role(lambda role: own_emb(role).start())
    for fetch in (own_tok, own_wg, own_wu, own_wd):
        fetch.start()

    stats[0] = jnp.zeros((8, 128), F32)
    stats[0, 2:6, :8] = pos_ref[...].astype(F32)
    stats[0, 6:7, :8] = cnt_ref[...].astype(F32)
    lists = pltpu.roll(stats[0], gslot * 8, 1)
    each_role(lambda role: own_emb(role).wait())
    own_tok.wait()
    pl.semaphore_wait(barrier, len(everyone))

    def e1_copy(role, k, back=False):
        part = (gb, pb)[role].at[slot_of(role, k if back else 0, back)]
        return copy(part, part, e1_s.at[k - 1], e1_r.at[k - 1], {"blk": ids_of(role)[k]})

    def e2_copy(role, o, i, back=False):
        part = (gb, pb)[role].at[slot_of(role, 4 * o + i if back else i, True)]
        return copy(part, part, e2_s.at[o - 1, i], e2_r.at[o - 1, i], {"blk": ids_of(role)[4 * o]})

    def fw_copy(role, k):
        part = (gb, pb)[role].at[slot_of(role, k, True)]
        return copy(part, part, fw_s.at[k], fw_r.at[k], {"tower": 1 - t})

    def emb_own(role):
        for k in (2, 1, 3):
            e1_copy(role, k).start()
        for o in range(1, count_of(role) // 4):
            e2_copy(role, o, 0).start()
        fw_copy(role, 0).start()

    def emb_inner(role):
        for i in (1, 3, 2):
            e1_copy(role, i, back=True).wait_recv()
            for o in range(1, count_of(role) // 4):
                e2_copy(role, o, i).start()
            fw_copy(role, i).start()

    def emb_outer(role):
        for i in (0, 1, 3, 2):
            for o in range(1, count_of(role) // 4):
                e2_copy(role, o, i, back=True).wait_recv()
                fw_copy(role, 4 * o + i).start()
        for k in range(count_of(1 - role)):
            fw_copy(1 - role, k).wait_recv()

    def za_copy(k):
        return copy(tok.at[0, x, yh], tok.at[k, x, yh], za_s.at[k - 1], za_r.at[k - 1], {"blk": premise_ids[k]})

    zb_parts = ((0, 4, 4, 1), (0, 4, 8, -1), (0, 2, 12, 2), (0, 1, 15, -2), (3, 1, 14, -2))

    def zb_copy(i):
        first, n, there, d = zb_parts[i]
        return copy(tok.at[pl.ds(first, n), x, yh, :, FIRST_SECOND], tok.at[pl.ds(there, n), x, yh, :, FIRST_SECOND],
                    zb_s.at[i], zb_r.at[i], {"blk": z_ids[d]})

    def yd_copy(row):
        part = tok.at[pl.ds(0, 4), x, row, :, THIRD]
        return copy(part, part, yd_s.at[0], yd_r.at[0], {"blk": y_id})

    def xd_copy(k, back=False):
        part = tok.at[pl.ds(0, 4), x_at[4 - k] if back else x, :, :, THIRD]
        return copy(part, part, xd_s.at[k - 1], xd_r.at[k - 1], {"blk": x_ids[k]})

    def zd_copy(i):
        first, n, there, d = zb_parts[i]
        return copy(tok.at[pl.ds(first, n), :, :, :, THIRD], tok.at[pl.ds(there, n), :, :, :, THIRD],
                    zd_s.at[i], zd_r.at[i], {"blk": z_ids[d]})

    def yb_copy(g, row):
        part = tok.at[pl.ds(4 * g, 4), x, row, :, FIRST]
        return copy(part, part, yb_s.at[g], yb_r.at[g], {"blk": y_id})

    def xc_copy(g, k, back=False):
        part = tok.at[pl.ds(4 * g, 4), x_at[4 - k] if back else x, yh, :, SECOND]
        return copy(part, part, xc_s.at[g, k - 1], xc_r.at[g, k - 1], {"blk": x_ids[k]})

    def xb_copy(g, k, back=False):
        part = tok.at[pl.ds(4 * g, 4), x_at[4 - k] if back else x, :, :, FIRST]
        return copy(part, part, xb_s.at[g, k - 1], xb_r.at[g, k - 1], {"blk": x_ids[k]})

    def yc_copy(g, row):
        part = tok.at[pl.ds(4 * g, 4), :, row, :, SECOND]
        return copy(part, part, yc_s.at[g], yc_r.at[g], {"blk": y_id})

    def tok_first():
        for k in (2, 1, 3):
            za_copy(k).start()
        zb_copy(3).start()

    def tok_near():
        for k in (1, 3, 2):
            za_copy(k).wait_recv()
        for i in (0, 1, 2, 4):
            zb_copy(i).start()
        yd_copy(yh).start()

    def tok_wide():
        yd_copy(1 - yh).wait_recv()
        for k in (1, 3, 2):
            xd_copy(k).start()

    def tok_far():
        for k in (1, 3, 2):
            xd_copy(k, back=True).wait_recv()
        for i in range(len(zb_parts)):
            zd_copy(i).start()

    def tok_second(g):
        for i, part in enumerate(zb_parts):
            if part[2] // 4 == g:
                zb_copy(i).wait_recv()
        for k in (1, 3, 2):
            xc_copy(g, k).start()
        yb_copy(g, yh).start()

    def tok_third(g):
        yb_copy(g, 1 - yh).wait_recv()
        for k in (1, 3, 2):
            xb_copy(g, k).start()
        for k in (1, 3, 2):
            xc_copy(g, k, back=True).wait_recv()
        yc_copy(g, yh).start()

    def tok_last(g):
        for k in (1, 3, 2):
            xb_copy(g, k, back=True).wait_recv()
        yc_copy(g, 1 - yh).wait_recv()
        for i, part in enumerate(zb_parts):
            if part[2] // 4 == g:
                zd_copy(i).wait_recv()

    each_role(emb_own)
    tok_first()
    each_role(emb_inner)
    tok_near()
    tok_second(0)
    each_role(emb_outer)
    tok_wide()

    goals = gb[...].reshape(NG * 8, W)
    premises = pb[...].reshape(NP * 8, W)
    s_own[...] = dot(premises, goals, NT)
    m1 = copy(s_own, s_in, m1_s.at[0], m1_r.at[0], {"mdl": 1 - m})
    m1.start()
    tok_second(1)

    m1.wait_recv()
    scores = (s_own[...] + s_in[...]) * SCORE_SCALE
    top = jnp.max(scores, axis=0, keepdims=True)
    total = jnp.sum(jnp.exp(scores - top), axis=0, keepdims=True)
    line = lax.broadcasted_iota(jnp.int32, (8, 128), 0)
    stats[0] = jnp.where(line == 0, top, jnp.where(line == 1, total, lists))

    def l1_copy(k):
        return copy(stats.at[0], stats.at[k], l1_s.at[k - 1], l1_r.at[k - 1], {"blk": goal_ids[k]})

    for k in range(1, NG):
        l1_copy(k).start()
    tok_second(2)
    tok_far()
    tok_third(0)

    def gate_copy(c):
        return copy(gsend.at[c], gin.at[c], gu_s.at[c], gu_r.at[c], {"mdl": 1 - m})

    def gate_chunk(c):
        rows = tok[4 * c:4 * c + 4].reshape(256, W)
        for lo, w in ((0, wg_ref), (U, wu_ref)):
            v = dot(w[...], rows, NT)
            gown[c, lo:lo + U] = v
            gsend[c, lo:lo + U] = v.astype(BF16)
        gate_copy(c).start()

    def spread(dtype):
        lane = lax.broadcasted_iota(jnp.int32, (8, 256), 1)
        sub = lax.broadcasted_iota(jnp.int32, (8, 256), 0)
        return jnp.where(lax.rem(lax.div(lane, 8), 8) == sub, 1.0, 0.0).astype(dtype)

    def act_chunk(c):
        gate_copy(c).wait_recv()
        g = gown[c, :U] + gin[c, :U].astype(F32)
        u = gown[c, U:] + gin[c, U:].astype(F32)
        s = 1.0 / (1.0 + jnp.exp(-g))
        a = g * s
        hidden = (a * u).astype(BF16)
        act1[c] = u * (s * (1.0 + g * (1.0 - s)))
        act2[c] = a
        part = dot(spread(BF16), hidden, NT)
        if c == 0:
            pool[:, U:] = jnp.zeros((8, 128 - U), F32)
            pool[:, :U] = part
        else:
            pool[:, :U] += part

    for k in range(1, NG):
        l1_copy(k).wait_recv()
    tops = [stats[k, 0:1] for k in range(NG)]
    peak = functools.reduce(jnp.maximum, tops)
    mass = functools.reduce(lambda p, q: p + q, [stats[k, 1:2] * jnp.exp(tops[k] - peak) for k in range(NG)])
    lse = peak + jnp.log(mass)
    codes = functools.reduce(lambda p, q: p + q, [stats[k] for k in range(NG)])
    count = codes[6:7]
    row = lax.broadcasted_iota(jnp.int32, (NP * 8, NG * 8), 0)
    member = lax.div(row, 8)
    premise_id = (blk_of(x, lax.div(member, 4), lax.rem(member, 4), zl) * 8 + lax.rem(row, 8)).astype(F32)
    weights = jnp.zeros((NP * 8, NG * 8), F32)
    for k in range(KPOS):
        hit = (codes[2 + k:3 + k] == premise_id) & (count > float(k))
        weights = weights + jnp.where(hit, 1.0, 0.0)
    coefficient = jnp.exp(scores - lse) - weights / count

    def mq_copy(role, k):
        src, dst = ((mbp, mbr), (mbp1, mbr1))[role]
        return copy(src.at[slot_of(role, k)], dst.at[k - 1], mq_s.at[k - 1], mq_r.at[k - 1], {"blk": ids_of(role)[k]})

    def r1_copy(role, k):
        first = (x_at, yh_at)[role][k] * 4
        return copy(go.at[pl.ds(first, 4)], rs1.at[k - 1], r1_s.at[k - 1], r1_r.at[k - 1], {"blk": ids_of(role)[4 * k]})

    def r2_copy(role, k):
        return copy(r2.at[(zl_at, zh_at)[role][k]], rs2.at[k - 1], r2_s.at[k - 1], r2_r.at[k - 1], {"blk": ids_of(role)[k]})

    def in_first(role):
        return (pslot, gslot)[role] == 0

    def start_sums(role):
        if role == 0:
            lhs = jnp.transpose(coefficient).astype(BF16)
            other = premises
        else:
            lhs = coefficient.astype(BF16)
            other = goals
        n = count_of(role)
        wide = W // n

        @pl.when(in_first(role))
        def _():
            target = (mbp, mbp1)[role]
            head = dot(lhs[:8], other, NN)
            for q in range(n):
                target[q] = head[:, q * wide:(q + 1) * wide]
            for k in range(1, n):
                mq_copy(role, k).start()

        go[:n] = dot(lhs, other, NN).astype(BF16).reshape(n, 8, W)
        for k in range(1, n // 4):
            r1_copy(role, k).start()

    each_role(start_sums)
    tok_second(3)
    tok_third(1)

    def slice_of(role, q):
        wide = W // count_of(role)
        return mb.at[:, pl.ds(pl.multiple_of(q * wide, wide), wide)]

    def mp_copy(role, k):
        part = slice_of(role, slot_of(role, 0))
        return copy(part, part, mp_s.at[k - 1], mp_r.at[0], {"blk": ids_of(1 - role)[k]})

    def ma_copy(role, k, back=False):
        part = slice_of(role, slot_of(role, k if back else 0, back))
        return copy(part, part, ma_s.at[k - 1], ma_r.at[k - 1], {"blk": ids_of(role)[k]})

    def spread_micro(role):
        n = count_of(role)
        wide = W // n
        me = slot_of(role, 0)
        own, got = ((mbp, mbr), (mbp1, mbr1))[role]

        @pl.when(in_first(role))
        def _():
            acc = own[me]
            for k in range(1, n):
                mq_copy(role, k).wait_recv()
                acc = acc + got[k - 1]
            mb[:, pl.ds(pl.multiple_of(me * wide, wide), wide)] = ((GRAD_SCALE * acc) / SEQ).astype(BF16)
            for k in range(1, count_of(1 - role)):
                mp_copy(role, k).start()

        @pl.when(jnp.logical_not(in_first(role)))
        def _():
            mp_copy(role, 1).wait_recv()

        for k in range(1, n):
            ma_copy(role, k).start()

    each_role(spread_micro)
    tok_third(2)

    def second_sums(role):
        acc = go[pl.ds((x, yh)[role] * 4, 4)].astype(F32)
        for k in range(1, count_of(role) // 4):
            r1_copy(role, k).wait_recv()
            acc = acc + rs1[k - 1].astype(F32)
        r2[...] = acc.astype(BF16)
        for k in range(1, 4):
            r2_copy(role, k).start()

    each_role(second_sums)
    own_wg.wait()
    own_wu.wait()
    own_wd.wait()
    tok_last(0)
    gate_chunk(0)

    def all_micro(role):
        for k in range(1, count_of(role)):
            ma_copy(role, k, back=True).wait_recv()

    each_role(all_micro)
    bk_own[:, :U] = dot(mb[...], wd_ref[...], NT)
    bk_own[:, U:] = jnp.zeros((8, 128 - U), F32)
    back = copy(bk_own, bk_in, d_s.at[0], d_r.at[0], {"mdl": 1 - m})
    back.start()
    tok_third(3)
    tok_last(1)
    gate_chunk(1)

    def last_sums(role):
        acc = r2[(zl, zh)[role]].astype(F32)
        for k in range(1, 4):
            r2_copy(role, k).wait_recv()
            acc = acc + rs2[k - 1].astype(F32)
        eg_ref[...] = GRAD_SCALE * acc

    each_role(last_sums)
    act_chunk(0)
    back.wait_recv()
    back_rows = thirds(jnp.transpose(bk_own[...] + bk_in[...])[:U])

    def back_chunk(c):
        wide = sum(dot(p, spread(BF16), NN) for p in back_rows)
        grads[:U, 256 * c:256 * c + 256] = (wide * act1[c]).astype(BF16)
        grads[U:, 256 * c:256 * c + 256] = (wide * act2[c]).astype(BF16)

    tok_last(2)
    gate_chunk(2)
    act_chunk(1)
    back_chunk(0)
    back_chunk(1)
    tok_last(3)
    gate_chunk(3)
    act_chunk(2)
    back_chunk(2)
    for j in range(W // TILE):
        cols = pl.ds(j * TILE, TILE)
        early[j] = dot(grads[:, :768], tok[:12, :, :, :, cols].reshape(768, TILE), NN)
    act_chunk(3)
    back_chunk(3)
    pooled = thirds(jnp.transpose(pool[...])[:U])
    gd_ref[...] = sum(dot(p, mb[...], NN) for p in pooled).astype(BF16)
    for j in range(W // TILE):
        cols = pl.ds(j * TILE, TILE)
        both = early[j] + dot(grads[:, 768:], tok[12:, :, :, :, cols].reshape(256, TILE), NN)
        gg_ref[:, cols] = both[:U].astype(BF16)
        gu_ref[:, cols] = both[U:].astype(BF16)

    def drain(role):
        n = count_of(role)
        for k in range(1, 4):
            e1_copy(role, k).wait_send()
            r2_copy(role, k).wait_send()
        for o in range(1, n // 4):
            for i in range(4):
                e2_copy(role, o, i).wait_send()
            r1_copy(role, o).wait_send()
        for k in range(n):
            fw_copy(role, k).wait_send()
        for k in range(1, n):
            ma_copy(role, k).wait_send()

        @pl.when(in_first(role))
        def _():
            for k in range(1, n):
                mq_copy(role, k).wait_send()
            for k in range(1, count_of(1 - role)):
                mp_copy(role, k).wait_send()

    each_role(drain)
    for k in (1, 2, 3):
        za_copy(k).wait_send()
        xd_copy(k).wait_send()
    for i in range(len(zb_parts)):
        zb_copy(i).wait_send()
        zd_copy(i).wait_send()
    yd_copy(yh).wait_send()
    for g in range(4):
        yb_copy(g, yh).wait_send()
        yc_copy(g, yh).wait_send()
        for k in (1, 2, 3):
            xb_copy(g, k).wait_send()
            xc_copy(g, k).wait_send()
    m1.wait_send()
    back.wait_send()
    for k in range(1, NG):
        l1_copy(k).wait_send()
    for c in range(4):
        gate_copy(c).wait_send()


def hand_over(eg, gg, gu, gd, eg_out, gg_out, gu_out, gd_out, sem):
    copies = [pltpu.make_async_copy(eg, eg_out.at[0], sem.at[0])]
    for j in range(W // TILE):
        cols = pl.ds(j * TILE, TILE)
        for v, out in ((gg, gg_out), (gu, gu_out), (gd, gd_out)):
            copies.append(pltpu.make_async_copy(v.at[:, cols], out.at[0, :, cols], sem.at[len(copies)]))
    for c in copies:
        c.start()
    for c in copies:
        c.wait()


def on_device(embeddings, pos_index, pos_count, hidden_in, w_gate, w_up, w_down):
    vmem = pl.BlockSpec(memory_space=pltpu.VMEM)
    hbm = pl.BlockSpec(memory_space=pltpu.HBM)
    dma = pltpu.SemaphoreType.DMA
    shapes = [(5,), (3,), (3,), (3, 4), (3, 4), (16,), (16,), (1,), (1,), (15,), (15,), (3,), (3,), (3,), (3,)]
    shapes += [(15,), (15,), (15,), (1,), (15,), (15,), (1,), (1,)]
    shapes += [(3,), (3,), (5,), (5,), (4,), (4,), (4, 3), (4, 3), (4,), (4,), (4, 3), (4, 3), (1,), (1,), (3,), (3,), (5,), (5,), (4,), (4,)]
    results = (jax.ShapeDtypeStruct((1, 8, W), F32),) + (jax.ShapeDtypeStruct((1, U, W), BF16),) * 3
    parts = pl.pallas_call(
        kernel,
        out_shape=tuple(pltpu.VMEM(v.shape[1:], v.dtype) for v in results),
        in_specs=[vmem] * 2 + [hbm] * 5,
        out_specs=(vmem,) * 4,
        scratch_shapes=[
            pltpu.VMEM((8, W), BF16),
            pltpu.VMEM((8, 128), F32),
            pltpu.VMEM((2 * U, 1024), BF16),
            pltpu.VMEM((NZ, NX, NYH, 8, W), BF16),
            pltpu.VMEM((W // TILE, 2 * U, TILE), F32),
            pltpu.VMEM((NG, 8, W), BF16),
            pltpu.VMEM((NP, 8, W), BF16),
            pltpu.VMEM((U, W), BF16),
            pltpu.VMEM((U, W), BF16),
            pltpu.VMEM((U, W), BF16),
            pltpu.VMEM((NP * 8, NG * 8), F32),
            pltpu.VMEM((NP * 8, NG * 8), F32),
            pltpu.VMEM((NG, 8, 128), F32),
            pltpu.VMEM((NG, 8, W), BF16),
            pltpu.VMEM((3, 4, 8, W), BF16),
            pltpu.VMEM((4, 8, W), BF16),
            pltpu.VMEM((3, 8, W), BF16),
            pltpu.VMEM((NG, 8, 128), F32),
            pltpu.VMEM((NG - 1, 8, 128), F32),
            pltpu.VMEM((NP, 8, 256), F32),
            pltpu.VMEM((NP - 1, 8, 256), F32),
            pltpu.VMEM((8, 128), F32),
            pltpu.VMEM((8, 128), F32),
            pltpu.VMEM((4, 2 * U, 256), F32),
            pltpu.VMEM((4, 2 * U, 256), BF16),
            pltpu.VMEM((4, 2 * U, 256), BF16),
            pltpu.VMEM((4, U, 256), F32),
            pltpu.VMEM((4, U, 256), F32),
        ]
        + [dma(s) for s in shapes],
        compiler_params=pltpu.CompilerParams(
            collective_id=0, has_side_effects=True, vmem_limit_bytes=60 * 1024 * 1024
        ),
    )(pos_index.T, pos_count[None], embeddings, hidden_in, w_gate, w_up, w_down)
    return pl.pallas_call(
        hand_over,
        out_shape=results,
        in_specs=[vmem] * 4,
        out_specs=(hbm,) * 4,
        scratch_shapes=[dma((13,))],
    )(*parts)


def solution(mesh):
    wide = P("tower", "blk", "mdl")
    return jax.shard_map(
        on_device,
        mesh=mesh,
        in_specs=(wide, P("blk", None), P("blk"), wide, wide, wide, wide),
        out_specs=(wide,) * 4,
        check_vma=False,
    )
```

time: 99.1 us -> 87.8 us (0.89)
  the two profiles are of different devices: /device:TPU:18 before, /device:TPU:1 now
where the time goes in v2:
time: 87.8 us; the launch traced here: 87.6 us
  Pallas kernels  84 us (96%)
  local copies, waits for them, and re-layouts  2.93 us (3%)
    pallas_call x1, Pallas kernels, on_device(): pl.pallas_call(kernel, out_shape=tuple((pltpu.VMEM(v.shape[1:], v.dtype)...  81.5 us
    unnamed x8, local copies, waits for them, and re-layouts  2.93 us
    pallas_call x1, Pallas kernels, on_device(): pl.pallas_call(hand_over, out_shape=results, in_specs=[vmem] * 4, out_spe...  2.52 us

profile of v2, /device:TPU:1, one launch (start us, length us, event | category | flops | bytes accessed | tf_op | source)
XLA Modules:
  0.0 87.6 jit_solution(12987041680937775822)
XLA Ops:
  0.6 81.5 %shard_map.102 = (f32[8,2048]{1,0:T(8,128)S(1)}, bf16[112,2048]{1,0:T(8,128)(2,1)S(1)}, bf16[112,2048]{1,0:T(8,128)(2,1)S(1)}, bf16[112,2048]{1,0:T(8,128)(2,1)S(1)}) custom-call(s32[4,8]{1,0:T(4,128)} %bitcast.2, s32[1,8]{1,0:T(1,128)} %bitcast.3, bf16[1,8,2048]{2,1,0:T(8,128)(2,1)} %emb_ref.1, bf16[1,8,2048]{2,1,0:T(8,128)(2,1)} %hid_ref.1, ...), custom_call_target="tpu_custom_call" | custom-call | tf_op jit(solution)/shard_map/pallas_call | solution.py:543
  82.1 0.0 copy-start
  82.1 0.8 copy-done
  82.9 0.0 copy-start.1
  82.9 0.8 copy-done.1
  83.7 0.0 copy-start.2
  83.7 0.8 copy-done.2
  84.5 0.0 copy-start.3
  84.5 0.6 copy-done.3
  85.1 2.5 %shard_map.103 = (f32[1,8,2048]{2,1,0:T(8,128)}, bf16[1,112,2048]{2,1,0:T(8,128)(2,1)}, bf16[1,112,2048]{2,1,0:T(8,128)(2,1)}, bf16[1,112,2048]{2,1,0:T(8,128)(2,1)}) custom-call(f32[8,2048]{1,0:T(8,128)} %copy-done.3, bf16[112,2048]{1,0:T(8,128)(2,1)} %copy-done, bf16[112,2048]{1,0:T(8,128)(2,1)} %copy-done.1, bf16[112,2048]{1,0:T(8,128)(2,1)} %copy-done.2), custom_call_target="tpu_custom_call" | custom-call | tf_op jit(solution)/shard_map/pallas_call | solution.py:583
Async XLA Ops:
  82.1 0.8 copy-start
  82.9 0.8 copy-start.1
  83.7 0.8 copy-start.2
  84.5 0.6 copy-start.3

commit v3 on v2

--- a/solution.py
+++ b/solution.py
@@ -44,7 +44,7 @@
     pos_ref, cnt_ref, emb_ref, hid_ref, wg_hbm, wu_hbm, wd_hbm,
     eg_ref, gg_ref, gu_ref, gd_ref,
     mb, pool, grads, tok, early,
-    gb, pb, wg_ref, wu_ref, wd_ref, s_own, s_in, stats, go, rs1, r2, rs2, mbp, mbr, mbp1, mbr1,
+    gb, pb, wgu_ref, wd_ref, s_own, s_in, stats, go, rs1, r2, rs2, mbp, mbr, mbp1, mbr1,
     bk_own, bk_in, gown, gsend, gin, act1, act2,
     loc, e1_s, e1_r, e2_s, e2_r, fw_s, fw_r, m1_s, m1_r, l1_s, l1_r, r1_s, r1_r, r2_s, r2_r,
     mq_s, mq_r, mp_s, mp_r, ma_s, ma_r, d_s, d_r,
@@ -115,8 +115,8 @@
         return pltpu.make_async_copy(emb_ref.at[0], (gb, pb)[role].at[slot_of(role, 0)], loc.at[0])
 
     own_tok = pltpu.make_async_copy(hid_ref.at[0], tok.at[0, x, yh], loc.at[1])
-    own_wg = pltpu.make_async_copy(wg_hbm.at[0], wg_ref, loc.at[2])
-    own_wu = pltpu.make_async_copy(wu_hbm.at[0], wu_ref, loc.at[3])
+    own_wg = pltpu.make_async_copy(wg_hbm.at[0], wgu_ref.at[pl.ds(0, U)], loc.at[2])
+    own_wu = pltpu.make_async_copy(wu_hbm.at[0], wgu_ref.at[pl.ds(U, U)], loc.at[3])
     own_wd = pltpu.make_async_copy(wd_hbm.at[0], wd_ref, loc.at[4])
     each_role(lambda role: own_emb(role).start())
     for fetch in (own_tok, own_wg, own_wu, own_wd):
@@ -263,7 +263,6 @@
     s_own[...] = dot(premises, goals, NT)
     m1 = copy(s_own, s_in, m1_s.at[0], m1_r.at[0], {"mdl": 1 - m})
     m1.start()
-    tok_second(1)
 
     m1.wait_recv()
     scores = (s_own[...] + s_in[...]) * SCORE_SCALE
@@ -277,8 +276,8 @@
 
     for k in range(1, NG):
         l1_copy(k).start()
+    tok_second(1)
     tok_second(2)
-    tok_far()
     tok_third(0)
 
     def gate_copy(c):
@@ -286,16 +285,15 @@
 
     def gate_chunk(c):
         rows = tok[4 * c:4 * c + 4].reshape(256, W)
-        for lo, w in ((0, wg_ref), (U, wu_ref)):
-            v = dot(w[...], rows, NT)
-            gown[c, lo:lo + U] = v
-            gsend[c, lo:lo + U] = v.astype(BF16)
+        both = dot(wgu_ref[...], rows, NT)
+        gown[c] = both
+        gsend[c] = both.astype(BF16)
         gate_copy(c).start()
 
-    def spread(dtype):
-        lane = lax.broadcasted_iota(jnp.int32, (8, 256), 1)
-        sub = lax.broadcasted_iota(jnp.int32, (8, 256), 0)
-        return jnp.where(lax.rem(lax.div(lane, 8), 8) == sub, 1.0, 0.0).astype(dtype)
+    def spread(rows):
+        lane = lax.broadcasted_iota(jnp.int32, (rows, 256), 1)
+        sub = lax.broadcasted_iota(jnp.int32, (rows, 256), 0)
+        return jnp.where(lax.rem(lax.div(lane, 8), 8) == lax.rem(sub, 8), 1.0, 0.0).astype(BF16)
 
     def act_chunk(c):
         gate_copy(c).wait_recv()
@@ -306,7 +304,7 @@
         hidden = (a * u).astype(BF16)
         act1[c] = u * (s * (1.0 + g * (1.0 - s)))
         act2[c] = a
-        part = dot(spread(BF16), hidden, NT)
+        part = dot(spread(8), hidden, NT)
         if c == 0:
             pool[:, U:] = jnp.zeros((8, 128 - U), F32)
             pool[:, :U] = part
@@ -369,6 +367,7 @@
 
     each_role(start_sums)
     tok_second(3)
+    tok_far()
     tok_third(1)
 
     def slice_of(role, q):
@@ -448,10 +447,10 @@
     each_role(last_sums)
     act_chunk(0)
     back.wait_recv()
-    back_rows = thirds(jnp.transpose(bk_own[...] + bk_in[...])[:U])
+    back_rows = jnp.concatenate(thirds(jnp.transpose(bk_own[...] + bk_in[...])[:U]), axis=1)
 
     def back_chunk(c):
-        wide = sum(dot(p, spread(BF16), NN) for p in back_rows)
+        wide = dot(back_rows, spread(24), NN)
         grads[:U, 256 * c:256 * c + 256] = (wide * act1[c]).astype(BF16)
         grads[U:, 256 * c:256 * c + 256] = (wide * act2[c]).astype(BF16)
 
@@ -467,16 +466,6 @@
     for j in range(W // TILE):
         cols = pl.ds(j * TILE, TILE)
         early[j] = dot(grads[:, :768], tok[:12, :, :, :, cols].reshape(768, TILE), NN)
-    act_chunk(3)
-    back_chunk(3)
-    pooled = thirds(jnp.transpose(pool[...])[:U])
-    gd_ref[...] = sum(dot(p, mb[...], NN) for p in pooled).astype(BF16)
-    for j in range(W // TILE):
-        cols = pl.ds(j * TILE, TILE)
-        both = early[j] + dot(grads[:, 768:], tok[12:, :, :, :, cols].reshape(256, TILE), NN)
-        gg_ref[:, cols] = both[:U].astype(BF16)
-        gu_ref[:, cols] = both[U:].astype(BF16)
-
     def drain(role):
         n = count_of(role)
         for k in range(1, 4):
@@ -516,8 +505,20 @@
     back.wait_send()
     for k in range(1, NG):
         l1_copy(k).wait_send()
-    for c in range(4):
+    for c in range(3):
         gate_copy(c).wait_send()
+
+    act_chunk(3)
+    back_chunk(3)
+    pooled = jnp.concatenate(thirds(jnp.transpose(pool[...])[:U]), axis=1)
+    gd_ref[...] = dot(pooled, jnp.concatenate([mb[...]] * 3, axis=0), NN).astype(BF16)
+    for j in range(W // TILE):
+        cols = pl.ds(j * TILE, TILE)
+        both = early[j] + dot(grads[:, 768:], tok[12:, :, :, :, cols].reshape(256, TILE), NN)
+        gg_ref[:, cols] = both[:U].astype(BF16)
+        gu_ref[:, cols] = both[U:].astype(BF16)
+
+    gate_copy(3).wait_send()
 
 
 def hand_over(eg, gg, gu, gd, eg_out, gg_out, gu_out, gd_out, sem):
@@ -553,8 +554,7 @@
             pltpu.VMEM((W // TILE, 2 * U, TILE), F32),
             pltpu.VMEM((NG, 8, W), BF16),
             pltpu.VMEM((NP, 8, W), BF16),
-            pltpu.VMEM((U, W), BF16),
-            pltpu.VMEM((U, W), BF16),
+            pltpu.VMEM((2 * U, W), BF16),
             pltpu.VMEM((U, W), BF16),
             pltpu.VMEM((NP * 8, NG * 8), F32),
             pltpu.VMEM((NP * 8, NG * 8), F32),

time: 87.8 us -> 84.6 us (0.964)
  Pallas kernels: 84 us -> 80.9 us
    pallas_call x1, Pallas kernels: 81.5 us -> 78.4 us  [on_device(): pl.pallas_call(kernel, out_shape=tuple((pltpu.VMEM(v.shape[1:], v.dtype)...]
where the time goes in v3:
time: 84.6 us; the launch traced here: 84.5 us
  Pallas kernels  80.9 us (96%)
  local copies, waits for them, and re-layouts  2.93 us (3%)
    pallas_call x1, Pallas kernels, on_device(): pl.pallas_call(kernel, out_shape=tuple((pltpu.VMEM(v.shape[1:], v.dtype)...  78.4 us
    unnamed x8, local copies, waits for them, and re-layouts  2.93 us
    pallas_call x1, Pallas kernels, on_device(): pl.pallas_call(hand_over, out_shape=results, in_specs=[vmem] * 4, out_spe...  2.52 us

profile of v3, /device:TPU:1, one launch (start us, length us, event | category | flops | bytes accessed | tf_op | source)
XLA Modules:
  0.0 84.5 jit_solution(7115581775200386317)
XLA Ops:
  0.6 78.4 %shard_map.102 = (f32[8,2048]{1,0:T(8,128)S(1)}, bf16[112,2048]{1,0:T(8,128)(2,1)S(1)}, bf16[112,2048]{1,0:T(8,128)(2,1)S(1)}, bf16[112,2048]{1,0:T(8,128)(2,1)S(1)}) custom-call(s32[4,8]{1,0:T(4,128)} %bitcast.2, s32[1,8]{1,0:T(1,128)} %bitcast.3, bf16[1,8,2048]{2,1,0:T(8,128)(2,1)} %emb_ref.1, bf16[1,8,2048]{2,1,0:T(8,128)(2,1)} %hid_ref.1, ...), custom_call_target="tpu_custom_call" | custom-call | tf_op jit(solution)/shard_map/pallas_call | solution.py:544
  79.0 0.0 copy-start
  79.0 0.8 copy-done
  79.8 0.0 copy-start.1
  79.8 0.8 copy-done.1
  80.5 0.0 copy-start.2
  80.5 0.8 copy-done.2
  81.3 0.0 copy-start.3
  81.3 0.6 copy-done.3
  81.9 2.5 %shard_map.103 = (f32[1,8,2048]{2,1,0:T(8,128)}, bf16[1,112,2048]{2,1,0:T(8,128)(2,1)}, bf16[1,112,2048]{2,1,0:T(8,128)(2,1)}, bf16[1,112,2048]{2,1,0:T(8,128)(2,1)}) custom-call(f32[8,2048]{1,0:T(8,128)} %copy-done.3, bf16[112,2048]{1,0:T(8,128)(2,1)} %copy-done, bf16[112,2048]{1,0:T(8,128)(2,1)} %copy-done.1, bf16[112,2048]{1,0:T(8,128)(2,1)} %copy-done.2), custom_call_target="tpu_custom_call" | custom-call | tf_op jit(solution)/shard_map/pallas_call | solution.py:583
Async XLA Ops:
  79.0 0.8 copy-start
  79.8 0.8 copy-start.1
  80.5 0.8 copy-start.2
  81.3 0.6 copy-start.3

commit v4 on v3

--- a/solution.py
+++ b/solution.py
@@ -20,8 +20,8 @@
 NN = (((1,), (0,)), ((), ()))
 
 W = 2048
-FIRST, SECOND, THIRD = pl.ds(0, 1024), pl.ds(1024, 512), pl.ds(1536, 512)
-FIRST_SECOND = pl.ds(0, 1536)
+FIRST, SECOND, THIRD = pl.ds(0, 1024), pl.ds(1024, 640), pl.ds(1664, 384)
+FIRST_SECOND = pl.ds(0, 1664)
 TILE = 512
 U = 112
 NX, NYH, NZ = 4, 2, 16

time: 84.6 us -> 84.5 us (level); the launches traced: 84.5 us -> 83.2 us
  Pallas kernels: 80.9 us -> 79.6 us
    pallas_call x1, Pallas kernels: 78.4 us -> 77 us  [on_device(): pl.pallas_call(kernel, out_shape=tuple((pltpu.VMEM(v.shape[1:], v.dtype)...]
where the time goes in v4:
time: 84.5 us; the launch traced here: 83.2 us
  Pallas kernels  79.6 us (94%)
  local copies, waits for them, and re-layouts  2.93 us (3%)
    pallas_call x1, Pallas kernels, on_device(): pl.pallas_call(kernel, out_shape=tuple((pltpu.VMEM(v.shape[1:], v.dtype)...  77 us
    unnamed x8, local copies, waits for them, and re-layouts  2.93 us
    pallas_call x1, Pallas kernels, on_device(): pl.pallas_call(hand_over, out_shape=results, in_specs=[vmem] * 4, out_spe...  2.52 us

profile of v4, /device:TPU:1, one launch (start us, length us, event | category | flops | bytes accessed | tf_op | source)
XLA Modules:
  0.0 83.2 jit_solution(2895700858656454328)
XLA Ops:
  0.6 77.0 %shard_map.102 = (f32[8,2048]{1,0:T(8,128)S(1)}, bf16[112,2048]{1,0:T(8,128)(2,1)S(1)}, bf16[112,2048]{1,0:T(8,128)(2,1)S(1)}, bf16[112,2048]{1,0:T(8,128)(2,1)S(1)}) custom-call(s32[4,8]{1,0:T(4,128)} %bitcast.2, s32[1,8]{1,0:T(1,128)} %bitcast.3, bf16[1,8,2048]{2,1,0:T(8,128)(2,1)} %emb_ref.1, bf16[1,8,2048]{2,1,0:T(8,128)(2,1)} %hid_ref.1, ...), custom_call_target="tpu_custom_call" | custom-call | tf_op jit(solution)/shard_map/pallas_call | solution.py:544
  77.7 0.0 copy-start
  77.7 0.8 copy-done
  78.5 0.0 copy-start.1
  78.5 0.8 copy-done.1
  79.2 0.0 copy-start.2
  79.2 0.8 copy-done.2
  80.0 0.0 copy-start.3
  80.0 0.6 copy-done.3
  80.6 2.5 %shard_map.103 = (f32[1,8,2048]{2,1,0:T(8,128)}, bf16[1,112,2048]{2,1,0:T(8,128)(2,1)}, bf16[1,112,2048]{2,1,0:T(8,128)(2,1)}, bf16[1,112,2048]{2,1,0:T(8,128)(2,1)}) custom-call(f32[8,2048]{1,0:T(8,128)} %copy-done.3, bf16[112,2048]{1,0:T(8,128)(2,1)} %copy-done, bf16[112,2048]{1,0:T(8,128)(2,1)} %copy-done.1, bf16[112,2048]{1,0:T(8,128)(2,1)} %copy-done.2), custom_call_target="tpu_custom_call" | custom-call | tf_op jit(solution)/shard_map/pallas_call | solution.py:583
Async XLA Ops:
  77.7 0.8 copy-start
  78.5 0.8 copy-start.1
  79.2 0.8 copy-start.2
  80.0 0.6 copy-start.3
